TPU v7x, 32 devices: a whole 2x2x4 slice. The times are simulated.
32 devices in a mesh: grp: 2 (over y), chan: 2 (over x), tm: 4 (over z), pol: 2 (over core).
Axes of the slice: x: 2, y: 2, z: 4, core: 2. Of those that a mesh axis runs over, the one named last changes fastest.
Arguments:
- voltages: bfloat16 [4, 2, 256, 32768], P('grp', 'pol', 'chan', 'tm'), parts along dimension 0, may hold values from -6 to 6
- taps_filter: float32 [16, 2048], replicated, may hold values from -1.5 to 1.5
- tile_a: int32 [14, 64], replicated, may hold values from 0 to 255
- tile_b: int32 [14, 64], replicated, may hold values from 0 to 255
- tile_owner: int32 [14], replicated, may hold values from 0 to 1, as said below
- tile_flags: int32 [14, 16], replicated, may hold values 0 or 1
Outputs:
- visibility: float32 [16, 256, 4, 2, 64, 128], P('pol', ('chan', 'tm'), 'grp'), parts along dimension 2
There are 2 independent parts, one for each index of `grp`. A program takes and returns all parts, laid end to end along the dimension named above; an argument that names none is the same for every part. Nothing has to cross between parts.
Inputs may be any that keep to these rules, and one draw needn't show every extreme that they name: `tile_owner`: one owner holds exactly 8 tiles and the other owner holds all the rest.
All inputs are finite; a program needn't handle non-finite values.
Results may differ from a plain program's by a relative error of at most 0.0035.
Values may be sent and summed in bfloat16 or wider, within the bound.
No kernel may reach another device: no remote copies, remote signals or barrier semaphores. Data moves between devices by JAX's collectives and lax.ppermute only.
A program may use at most 128 MiB of HBM per device.

v0:
```python
import math

import jax
import jax.numpy as jnp
import numpy as np
from jax import lax
from jax.experimental import pallas as pl
from jax.experimental.pallas import tpu as pltpu
from jax.sharding import PartitionSpec as P

AVG = 8
CAP = 8
RADIX = 16
LANES = 128
ROWS = 16


radix_first = 32


def from_behind(value, axis, steps):
    count = lax.axis_size(axis)
    first, last = (max(0, -steps), min(count, count - steps))
    return lax.ppermute(value, axis, [(source, source + steps) for source in range(first, last)])


def fourier(filtered):
    length = filtered.shape[-1]
    second = length // radix_first
    exact_mode = lax.Precision.HIGHEST
    grid = filtered.reshape(filtered.shape[:-1] + (radix_first, second))
    outer = jnp.arange(radix_first, dtype=jnp.int32)
    inner = jnp.arange(second, dtype=jnp.int32)
    phase_one = (
        2.0
        * math.pi
        / radix_first
        * (outer[:, None] * outer[None, :] % radix_first).astype(jnp.float32)
    )
    phase_twist = 2.0 * math.pi / length * (outer[:, None] * inner[None, :]).astype(jnp.float32)
    phase_two = (
        2.0 * math.pi / second * (inner[:, None] * inner[None, :] % second).astype(jnp.float32)
    )
    cos_one, sin_one = (jnp.cos(phase_one), jnp.sin(phase_one))
    cos_twist, sin_twist = (jnp.cos(phase_twist), jnp.sin(phase_twist))
    cos_two, sin_two = (jnp.cos(phase_two), jnp.sin(phase_two))
    first_form = "fk,stkj->stfj"
    section_re = jnp.einsum(first_form, cos_one, grid[0], precision=exact_mode) + jnp.einsum(
        first_form, sin_one, grid[1], precision=exact_mode
    )
    section_im = jnp.einsum(first_form, cos_one, grid[1], precision=exact_mode) - jnp.einsum(
        first_form, sin_one, grid[0], precision=exact_mode
    )
    turned_re = section_re * cos_twist + section_im * sin_twist
    turned_im = section_im * cos_twist - section_re * sin_twist
    second_form = "gj,stfj->stgf"
    final_re = jnp.einsum(second_form, cos_two, turned_re, precision=exact_mode) + jnp.einsum(
        second_form, sin_two, turned_im, precision=exact_mode
    )
    final_im = jnp.einsum(second_form, cos_two, turned_im, precision=exact_mode) - jnp.einsum(
        second_form, sin_two, turned_re, precision=exact_mode
    )
    joined = jnp.stack([final_re, final_im]).reshape(filtered.shape)
    return joined * (1.0 / math.sqrt(length))


def correlate(full, rows_a, rows_b, flags, group_count):
    depth = full.shape[4]
    weight = jnp.tile(flags.astype(jnp.bfloat16), depth // flags.shape[0])
    left_rows = jnp.take(full, rows_a, axis=2) * weight
    right_rows = jnp.take(full, rows_b, axis=2)
    stacked_left = jnp.stack(
        [
            jnp.concatenate([left_rows[0], left_rows[1]], axis=-1),
            jnp.concatenate([left_rows[1], -left_rows[0]], axis=-1),
        ]
    )
    joined_right = jnp.concatenate([right_rows[0], right_rows[1]], axis=-1)
    result = jnp.einsum(
        "rpank,qbnk->nrpaqb", stacked_left, joined_right, preferred_element_type=jnp.float32
    )
    width = rows_a.shape[0]
    return result.reshape(group_count, 2, 2, width, 2 * width) * (1.0 / depth)


def on_device_any(voltages, taps_filter, tile_a, tile_b, tile_owner, tile_flags):
    history = taps_filter.shape[0] - 1
    length = taps_filter.shape[1]
    stations = voltages.shape[2]
    frames = voltages.shape[3] // length
    local_blocks = voltages.reshape(2, stations, frames, length)
    hop_count = -(-history // frames)
    sending = local_blocks
    extended = local_blocks
    for hop_index in range(hop_count):
        sending = from_behind(sending, "tm", 1)
        extended = jnp.concatenate([sending, extended], axis=2)
    extended = extended[:, :, extended.shape[2] - history - frames :]
    filtered = jnp.zeros((2, stations, frames, length), jnp.float32)
    for tap_index in range(history + 1):
        start = history - tap_index
        filtered = filtered + taps_filter[tap_index] * extended[
            :, :, start : start + frames
        ].astype(jnp.float32)
    spectra = fourier(filtered).astype(jnp.bfloat16)
    chan_count = lax.axis_size("chan")
    time_count = lax.axis_size("tm")
    narrow = length // (chan_count * time_count)
    outgoing = spectra.reshape(2, stations, frames, chan_count, time_count, narrow)
    outgoing = outgoing.transpose(0, 3, 4, 5, 1, 2)
    flat = outgoing.reshape(2, chan_count * time_count, narrow, stations * frames)
    moved = lax.all_to_all(flat, ("chan", "tm"), split_axis=1, concat_axis=1, tiled=True)
    moved = moved.reshape(2, chan_count, time_count, narrow, stations, frames)
    bands = narrow // AVG
    every_station = chan_count * stations
    spectra_count = time_count * frames
    arranged = moved.transpose(0, 1, 4, 3, 2, 5).reshape(
        2, 1, every_station, bands, AVG * spectra_count
    )
    full = lax.all_gather(arranged, "pol", axis=1, tiled=True)
    position = lax.axis_index("pol")
    width = tile_a.shape[1]
    capacity = CAP
    held = tile_owner == position
    listed = jnp.nonzero(held, size=capacity, fill_value=0)[0].astype(jnp.int32)
    tally = jnp.sum(held.astype(jnp.int32))
    initial = jnp.zeros((capacity, bands, 2, 2, width, 2 * width), jnp.float32)

    def fill_slot(slot, results):
        chosen_tile = listed[slot]
        return results.at[slot].set(
            correlate(
                full, tile_a[chosen_tile], tile_b[chosen_tile], tile_flags[chosen_tile], bands
            )
        )

    visibility = lax.fori_loop(0, tally, fill_slot, initial)
    return visibility


def fourier_tables(length):
    low = np.arange(RADIX)
    lane = np.arange(LANES)
    turn = 2.0 * np.pi / length * np.outer(low, lane)
    twiddle = np.stack([np.cos(turn), np.sin(turn)]).astype(np.float32)
    angle = 2.0 * np.pi / LANES * (np.outer(lane, lane) % LANES)
    cos, sin = np.cos(angle) / math.sqrt(length), np.sin(angle) / math.sqrt(length)
    matrix = np.block([[cos, sin], [-sin, cos]]).astype(np.float32)
    high = matrix.astype(jnp.bfloat16)
    rest = (matrix - high.astype(np.float32)).astype(jnp.bfloat16)
    return twiddle, np.stack([high, rest])


def butterflies(values):
    count = len(values)
    if count == 1:
        return values
    even, odd = butterflies(values[0::2]), butterflies(values[1::2])
    first, second = [], []
    for index in range(count // 2):
        (a, b), (c, d) = even[index], odd[index]
        if index == 0:
            e, f = c, d
        elif 4 * index == count:
            e, f = d, -c
        elif 8 * index == count:
            root = math.sqrt(0.5)
            e, f = (c + d) * root, (d - c) * root
        elif 8 * index == 3 * count:
            root = math.sqrt(0.5)
            e, f = (d - c) * root, -(c + d) * root
        else:
            turn = 2.0 * math.pi * index / count
            cos, sin = math.cos(turn), math.sin(turn)
            e, f = c * cos + d * sin, d * cos - c * sin
        first.append((a + e, b + f))
        second.append((a - e, b - f))
    return first + second


def channelise_kernel(
    frames, x_ref, taps_ref, twiddle_ref, matrix_ref, out_ref, fil_ref, zr_ref, zi_ref, w_ref
):
    sources = x_ref.shape[0]
    spectra = sources * frames
    length = taps_ref.shape[1]
    taps = taps_ref.shape[0]
    depth = RADIX * spectra
    z_refs = (zr_ref, zi_ref)

    @pl.loop(0, RADIX)
    def _(section):
        at = pl.multiple_of(section * LANES, LANES)
        weights = [taps_ref[pl.ds(m, 1), pl.ds(at, LANES)] for m in range(taps)]
        for part in range(2):
            blocks = []
            for t in range(spectra):
                lane = pl.multiple_of((t % frames) * length + section * LANES, LANES)
                blocks.append(x_ref[t // frames, part, :, pl.ds(lane, LANES)].astype(jnp.float32))
            for t in range(spectra):
                total = weights[0] * blocks[t]
                for m in range(1, min(t + 1, taps)):
                    total = total + weights[m] * blocks[t - m]
                fil_ref[section, t, part] = total

    @pl.loop(0, spectra)
    def _(t):
        for half in range(ROWS // 8):
            values = [
                tuple(fil_ref[section, t, part, pl.ds(half * 8, 8), :] for part in range(2))
                for section in range(RADIX)
            ]
            for low, (re, im) in enumerate(butterflies(values)):
                if low:
                    cos = twiddle_ref[0, pl.ds(low, 1), :]
                    sin = twiddle_ref[1, pl.ds(low, 1), :]
                    re, im = re * cos + im * sin, im * cos - re * sin
                rows = pl.ds(half * 8 * depth + low * spectra + t, 8, stride=depth)
                zr_ref[rows, :] = re
                zi_ref[rows, :] = im

    form = (((1,), (1,)), ((), ()))
    high_matrix, low_matrix = matrix_ref[0], matrix_ref[1]
    halves = depth // LANES

    @pl.loop(0, ROWS)
    def _(station):
        rows = pl.ds(pl.multiple_of(station * depth, depth), depth)
        value = jnp.concatenate([ref[rows, :] for ref in z_refs], axis=1)
        high = value.astype(jnp.bfloat16)
        rest = (value - high.astype(jnp.float32)).astype(jnp.bfloat16)
        total = lax.dot_general(high_matrix, high, form, preferred_element_type=jnp.float32)
        total += lax.dot_general(high_matrix, rest, form, preferred_element_type=jnp.float32)
        total += lax.dot_general(low_matrix, high, form, preferred_element_type=jnp.float32)
        for half in range(halves):
            for part in range(2):
                rows = pl.ds((half * 2 + part) * ROWS + station, LANES, stride=halves * 2 * ROWS)
                w_ref[rows, :] = total[
                    part * LANES : (part + 1) * LANES, half * LANES : (half + 1) * LANES
                ]

    piece = 256

    @pl.loop(0, out_ref.shape[0] // piece)
    def _(index):
        rows = pl.ds(pl.multiple_of(index * piece, piece), piece)
        out_ref[rows, :] = w_ref[rows, :].astype(jnp.bfloat16)


def channelise(blocks, taps_filter, tables, frames):
    sources = blocks.shape[0]
    length = taps_filter.shape[1]
    spectra = sources * frames
    twiddle, matrix = tables
    out_rows = length // AVG * 2 * ROWS
    whole = pl.BlockSpec(memory_space=pltpu.VMEM)
    flat = pl.pallas_call(
        lambda *refs: channelise_kernel(frames, *refs),
        out_shape=jax.ShapeDtypeStruct((out_rows, LANES), jnp.bfloat16),
        in_specs=[whole] * 4,
        out_specs=whole,
        scratch_shapes=[
            pltpu.VMEM((RADIX, spectra, 2, ROWS, LANES), jnp.float32),
            pltpu.VMEM((ROWS * RADIX * spectra, LANES), jnp.float32),
            pltpu.VMEM((ROWS * RADIX * spectra, LANES), jnp.float32),
            pltpu.VMEM((out_rows, LANES), jnp.float32),
        ],
        compiler_params=pltpu.CompilerParams(vmem_limit_bytes=40 * 2**20),
        cost_estimate=pl.CostEstimate(
            flops=9 * 10**9, bytes_accessed=4 * 2**20, transcendentals=0
        ),
        name="channelise",
    )(blocks, taps_filter, jnp.asarray(twiddle), jnp.asarray(matrix))
    return flat.reshape(length // AVG, 2, ROWS, LANES)


def correlate_kernel(chunks, width, *refs):
    sel_ref, weight_ref = refs[:2]
    x_refs = refs[2 : 2 + chunks]
    out_ref, x_all, rows_all = refs[2 + chunks :]
    tiles = out_ref.shape[0]
    chunk_rows = x_all.shape[0] // chunks
    for chunk, x_ref in enumerate(x_refs):
        for pol in range(2):
            for part in range(2):
                x_all[
                    chunk * chunk_rows : (chunk + 1) * chunk_rows,
                    (pol * 2 + part) * LANES : (pol * 2 + part + 1) * LANES,
                ] = x_ref[pol, :, 0, part].reshape(chunk_rows, LANES)
    step = 2
    for first in range(0, tiles, step):
        rows = slice(first * 2 * width, (first + step) * 2 * width)
        picked = jnp.dot(sel_ref[rows, :], x_all[...], preferred_element_type=jnp.float32)
        for tile in range(first, first + step):
            base = (tile - first) * 2 * width
            left = picked[base : base + width] * weight_ref[pl.ds(tile, 1), :]
            right = picked[base + width : base + 2 * width]
            rows_all[tile * 2 * width : tile * 2 * width + width, :] = left.astype(jnp.bfloat16)
            rows_all[tile * 2 * width + width : (tile + 1) * 2 * width, :] = right.astype(
                jnp.bfloat16
            )
    form = (((1,), (1,)), ((), ()))
    for tile in range(tiles):
        at = tile * 2 * width
        left = jnp.concatenate(
            [rows_all[at : at + width, pol * 2 * LANES : (pol + 1) * 2 * LANES] for pol in range(2)]
        )
        at += width
        right = jnp.concatenate(
            [rows_all[at : at + width, pol * 2 * LANES : (pol + 1) * 2 * LANES] for pol in range(2)]
        )
        turned = jnp.concatenate([-right[:, LANES:], right[:, :LANES]], axis=1)
        both = jnp.concatenate([right, turned])
        result = lax.dot_general(left, both, form, preferred_element_type=jnp.float32)
        for part in range(2):
            out_ref[tile, 0, part] = result[:, part * 2 * width : (part + 1) * 2 * width].reshape(
                2, width, 2 * width
            )


def correlate_tiles(chunks, select, weight, width):
    sources, bands = chunks[0].shape[1:3]
    tiles = weight.shape[0]
    block = (2, sources, 1, 2, ROWS, LANES)
    station_rows = len(chunks) * sources * ROWS
    return pl.pallas_call(
        lambda *refs: correlate_kernel(len(chunks), width, *refs),
        grid=(bands,),
        out_shape=jax.ShapeDtypeStruct((tiles, bands, 2, 2, width, 2 * width), jnp.float32),
        in_specs=[
            pl.BlockSpec(select.shape, lambda g: (0, 0)),
            pl.BlockSpec(weight.shape, lambda g: (0, 0)),
        ]
        + [pl.BlockSpec(block, lambda g: (0, 0, g, 0, 0, 0))] * len(chunks),
        out_specs=pl.BlockSpec(
            (tiles, 1, 2, 2, width, 2 * width), lambda g: (0, g, 0, 0, 0, 0)
        ),
        scratch_shapes=[
            pltpu.VMEM((station_rows, 4 * LANES), jnp.bfloat16),
            pltpu.VMEM((tiles * 2 * width, 4 * LANES), jnp.bfloat16),
        ],
        compiler_params=pltpu.CompilerParams(vmem_limit_bytes=32 * 2**20),
        cost_estimate=pl.CostEstimate(
            flops=13 * 10**9, bytes_accessed=42 * 2**20, transcendentals=0
        ),
        name="correlate",
    )(select, weight, *chunks)


def tile_tables(tile_a, tile_b, tile_owner, tile_flags, row_of):
    tiles = tile_owner.shape[0]
    held = tile_owner == lax.axis_index("pol")
    order = jnp.arange(tiles, dtype=jnp.int32)
    rank = jnp.sum((held[None, :] & (order[None, :] < order[:, None])).astype(jnp.int32), axis=1)
    slots = jnp.arange(CAP, dtype=jnp.int32)
    pick = (held[None, :] & (rank[None, :] == slots[:, None])).astype(jnp.int32)
    sides = jnp.stack([row_of(tile_a), row_of(tile_b)], axis=1) + 1
    rows = jnp.sum(pick[:, :, None, None] * sides[None], axis=1) - 1
    flags = jnp.sum(pick[:, :, None] * tile_flags[None], axis=1).astype(jnp.float32)
    return rows, flags


def on_device_chunks(voltages, taps_filter, tile_a, tile_b, tile_owner, tile_flags):
    length = taps_filter.shape[1]
    stations = voltages.shape[2]
    frames = voltages.shape[3] // length
    chan_count, time_count = lax.axis_size("chan"), lax.axis_size("tm")
    owners = chan_count * time_count
    chunk_count = stations // (time_count * ROWS)
    width = tile_a.shape[1]
    bands = length // AVG // owners
    tables = fourier_tables(length)

    def row_of(station):
        column = station // stations
        rest = station % stations
        block, inside = rest // (chunk_count * ROWS), rest % (chunk_count * ROWS)
        source = column * time_count + block
        return (inside // ROWS) * (owners * ROWS) + source * ROWS + inside % ROWS

    rows, flags = tile_tables(tile_a, tile_b, tile_owner, tile_flags, row_of)
    total_rows = chunk_count * owners * ROWS
    select = (rows[..., None] == jnp.arange(total_rows, dtype=jnp.int32)).astype(jnp.bfloat16)
    select = select.reshape(CAP * 2 * width, total_rows)
    depth = AVG * time_count * frames
    weight = jnp.tile(flags * (1.0 / depth), (1, 4 * AVG))

    pieces = voltages.reshape(2, time_count, chunk_count, ROWS, frames * length)
    received = []
    for chunk in range(chunk_count):
        sending = pieces[:, :, chunk].transpose(1, 0, 2, 3)
        blocks = lax.all_to_all(sending, "tm", split_axis=0, concat_axis=0, tiled=True)
        spectra = channelise(blocks, taps_filter, tables, frames)
        spectra = spectra.reshape(owners, bands, 2, ROWS, LANES)
        moved = lax.all_to_all(spectra, ("chan", "tm"), split_axis=0, concat_axis=0, tiled=True)
        received.append(lax.all_gather(moved, "pol", axis=0, tiled=False))
    return correlate_tiles(received, select, weight, width)


def on_device(voltages, taps_filter, tile_a, tile_b, tile_owner, tile_flags):
    taps, length = taps_filter.shape
    frames = voltages.shape[3] // length
    time_count = lax.axis_size("tm")
    fits = (
        length == RADIX * LANES
        and AVG * time_count * frames == LANES
        and voltages.shape[2] % (time_count * ROWS) == 0
        and 2 * tile_a.shape[1] == LANES
    )
    form = on_device_chunks if fits else on_device_any
    return form(voltages, taps_filter, tile_a, tile_b, tile_owner, tile_flags)


def solution(mesh):
    return jax.shard_map(
        on_device,
        mesh=mesh,
        in_specs=(P("grp", "pol", "chan", "tm"), P(), P(), P(), P(), P()),
        out_specs=P("pol", ("chan", "tm"), "grp", None, None, None),
        check_vma=False,
    )
```

profile of v0, /device:TPU:11, one launch (start us, length us, event | category | flops | bytes accessed | tf_op | source)
XLA Modules:
  0.0 302.6 jit_solution(432925609826643105)
XLA Ops:
  6.5 4.0 %fusion.34 = (bf16[2,4,1,16,8192]{4,3,2,1,0:T(8,128)(2,1)S(1)}, bf16[2,4,1,16,8192]{4,3,2,1,0:T(8,128)(2,1)}) fusion(bf16[2,4,2,16,8192]{4,3,2,1,0:T(8,128)(2,1)} %bitcast.24), kind=kLoop, calls=%fused_computation.82 | loop fusion | bytes 8388608 | tf_op jit(solution)/shard_map/slice | solution.py:391
  10.5 0.1 copy.27
  10.7 50.2 %all_to_all.20.refs_0_ = bf16[4,2,16,8192]{3,2,1,0:T(8,128)(2,1)S(1)} all-to-all(bf16[4,2,16,8192]{3,2,1,0:T(8,128)(2,1)S(1)} %bitcast.23), channel_id=1, replica_groups=mesh['grp'=2,'chan'=2,'tm'=4,'pol'=2] {'tm'}, dimensions={0} | all-to-all | bytes 4194304 | tf_op jit(solution)/shard_map/all_to_all | solution.py:392
  60.9 16.2 %channelise.3 = bf16[8192,128]{1,0:T(8,128)(2,1)} custom-call(bf16[4,2,16,8192]{3,2,1,0:T(8,128)(2,1)S(1)} %all_to_all.20.refs_0_, f32[16,2048]{1,0:T(8,128)S(1)} %copy-done.2, f32[2,16,128]{2,1,0:T(8,128)S(1)} %copy-done.4, bf16[2,256,256]{2,1,0:T(8,128)(2,1)S(1)} %copy-done.3), custom_call_target="tpu_custom_call" | custom-call | flops 8999999488 | bytes 4194304 | tf_op jit(solution)/shard_map/channelise/pallas_call | solution.py:257
  77.1 6.0 %all-to-all-start.3 = ((bf16[8,32,2,16,128]{4,3,2,1,0:T(8,128)(2,1)}), bf16[8,32,2,16,128]{4,3,2,1,0:T(8,128)(2,1)S(1)}, u32[]{:S(2)}, u32[]{:S(2)}) async-start(bf16[8,32,2,16,128]{4,3,2,1,0:T(8,128)(2,1)} %bitcast.9), calls=%async_computation.3 | async-start | bytes 4194304 | tf_op jit(solution)/shard_map/all_to_all | solution.py:395
  83.1 3.1 %copy.28 = bf16[2,4,1,16,8192]{4,3,0,1,2:T(8,128)(2,1)} copy(bf16[2,4,1,16,8192]{4,3,2,1,0:T(8,128)(2,1)} %get-tuple-element.6) | data formatting | bytes 4194304
  86.2 42.6 %all-to-all-done.3 = bf16[8,32,2,16,128]{4,3,2,1,0:T(8,128)(2,1)S(1)} async-done(((bf16[8,32,2,16,128]{4,3,2,1,0:T(8,128)(2,1)}), bf16[8,32,2,16,128]{4,3,2,1,0:T(8,128)(2,1)S(1)}, u32[]{:S(2)}, u32[]{:S(2)}) %all-to-all-start.3) | async-done | bytes 2097184 | tf_op jit(solution)/shard_map/all_to_all | solution.py:395
  128.9 1.3 copy-done.5
  130.2 4.6 %all-to-all-start = ((bf16[4,2,16,8192]{3,2,1,0:T(8,128)(2,1)}), bf16[4,2,16,8192]{3,2,1,0:T(8,128)(2,1)S(1)}, u32[]{:S(2)}, u32[]{:S(2)}) async-start(bf16[4,2,16,8192]{3,2,1,0:T(8,128)(2,1)} %bitcast.22), calls=%async_computation | async-start | bytes 4194304 | tf_op jit(solution)/shard_map/all_to_all | solution.py:392
  134.8 0.7 all-gather.7.cloned.1.call-update
  135.6 42.1 %all-to-all-done.refs_0_ = bf16[4,2,16,8192]{3,2,1,0:T(8,128)(2,1)S(1)} async-done(((bf16[4,2,16,8192]{3,2,1,0:T(8,128)(2,1)}), bf16[4,2,16,8192]{3,2,1,0:T(8,128)(2,1)S(1)}, u32[]{:S(2)}, u32[]{:S(2)}) %all-to-all-start) | async-done | bytes 2097184 | tf_op jit(solution)/shard_map/all_to_all | solution.py:392
  177.7 14.9 %channelise.2 = bf16[8192,128]{1,0:T(8,128)(2,1)S(1)} custom-call(bf16[4,2,16,8192]{3,2,1,0:T(8,128)(2,1)S(1)} %all-to-all-done.refs_0_, f32[16,2048]{1,0:T(8,128)S(1)} %copy-done.2, f32[2,16,128]{2,1,0:T(8,128)S(1)} %copy-done.4, bf16[2,256,256]{2,1,0:T(8,128)(2,1)S(1)} %copy-done.3), custom_call_target="tpu_custom_call" | custom-call | flops 8999999488 | bytes 4194304 | tf_op jit(solution)/shard_map/channelise/pallas_call | solution.py:257
  192.6 53.9 %all_to_all.21 = bf16[8,32,2,16,128]{4,3,2,1,0:T(8,128)(2,1)} all-to-all(bf16[8,32,2,16,128]{4,3,2,1,0:T(8,128)(2,1)S(1)} %bitcast.19), channel_id=1, replica_groups=mesh['grp'=2,'chan'=2,'tm'=4,'pol'=2] {'chan','tm'}, dimensions={0} | all-to-all | bytes 4194304 | tf_op jit(solution)/shard_map/all_to_all | solution.py:395
  246.5 0.7 copy-done.7
  247.3 0.1 convert_reduce_fusion
  247.5 0.1 multiply_reduce_fusion
  247.6 0.1 sub.39
  247.7 0.1 multiply_reduce_fusion.1
  247.8 0.1 tile.10.refs_1_
  247.9 0.2 fusion.refs_0_
  248.2 14.5 %all-gather.5.cloned.1.call-done = bf16[16,32,2,16,128]{4,3,2,1,0:T(8,128)(2,1)} async-done(((bf16[8,32,2,16,128]{4,3,2,1,0:T(8,128)(2,1)}), bf16[16,32,2,16,128]{4,3,2,1,0:T(8,128)(2,1)}) %all-gather.5.cloned.1.call-update) | async-done | bytes 4194320 | tf_op jit(solution)/shard_map/all_gather | solution.py:396
  262.6 2.2 copy-done
  264.8 2.2 copy-done.1
  267.0 28.8 %correlate.1 = f32[8,32,2,2,64,128]{5,4,3,2,1,0:T(8,128)} custom-call(bf16[1024,256]{1,0:T(8,128)(2,1)S(1)} %fusion.refs_0_, f32[8,512]{1,0:T(8,128)S(1)} %tile.10.refs_1_, bf16[2,8,32,2,16,128]{5,4,3,2,1,0:T(8,128)(2,1)S(1)} %bitcast.21, bf16[2,8,32,2,16,128]{5,4,3,2,1,0:T(8,128)(2,1)S(1)} %bitcast.20), custom_call_target="tpu_custom_call" | custom-call | flops 12999999488 | bytes 44040192 | tf_op jit(solution)/shard_map/correlate/pallas_call | solution.py:326
  (29 shorter events, 0.3 us)
Async XLA Ops:
  10.7 50.2 %copy-start.2 = (f32[16,2048]{1,0:T(8,128)S(1)}, f32[16,2048]{1,0:T(8,128)}, u32[]{:S(2)}) copy-start(f32[16,2048]{1,0:T(8,128)} %refs_1_.3) | copy-start | bytes 393220
  10.7 50.2 %copy-start.3 = (bf16[2,256,256]{2,1,0:T(8,128)(2,1)S(1)}, bf16[2,256,256]{2,1,0:T(8,128)(2,1)}, u32[]{:S(2)}) copy-start(bf16[2,256,256]{2,1,0:T(8,128)(2,1)} %constant.122.clone.refs_3_) | copy-start | bytes 786436
  10.7 50.2 %copy-start.4 = (f32[2,16,128]{2,1,0:T(8,128)S(1)}, f32[2,16,128]{2,1,0:T(8,128)}, u32[]{:S(2)}) copy-start(f32[2,16,128]{2,1,0:T(8,128)} %constant.121.clone.refs_2_) | copy-start | bytes 49156
  77.1 51.8 %all-to-all-start.3 = ((bf16[8,32,2,16,128]{4,3,2,1,0:T(8,128)(2,1)}), bf16[8,32,2,16,128]{4,3,2,1,0:T(8,128)(2,1)S(1)}, u32[]{:S(2)}, u32[]{:S(2)}) async-start(bf16[8,32,2,16,128]{4,3,2,1,0:T(8,128)(2,1)} %bitcast.9), calls=%async_computation.3 | async-start | bytes 4194304 | tf_op jit(solution)/shard_map/all_to_all | solution.py:395
  128.9 1.3 copy-start.5
  130.2 47.5 %all-to-all-start = ((bf16[4,2,16,8192]{3,2,1,0:T(8,128)(2,1)}), bf16[4,2,16,8192]{3,2,1,0:T(8,128)(2,1)S(1)}, u32[]{:S(2)}, u32[]{:S(2)}) async-start(bf16[4,2,16,8192]{3,2,1,0:T(8,128)(2,1)} %bitcast.22), calls=%async_computation | async-start | bytes 4194304 | tf_op jit(solution)/shard_map/all_to_all | solution.py:392
  134.8 113.4 %all-gather.7.cloned.1.call-start = ((), (), s32[]{:S(2)}) async-start(), calls=%async_computation.5 | async-start | bytes 6291456 | tf_op jit(solution)/shard_map/all_gather | solution.py:396
  135.5 127.1 %all-gather.5.cloned.1.call-start = ((), (), s32[]{:S(2)}) async-start(), calls=%async_computation.4 | async-start | bytes 6291456 | tf_op jit(solution)/shard_map/all_gather | solution.py:396
  246.5 0.7 copy-start.7
  246.5 0.7 copy-start.8
  246.5 0.8 copy-start.9
  246.5 1.2 copy-start.6
  262.6 2.2 copy-start
  264.8 2.2 copy-start.1
Sparse Core Ops, SparseCore 0:
  137.2 17.2 all-gather.6
  246.6 15.9 all-gather.4
where the time goes:
time: 304 us; the launch traced here: 303 us
  blocking collectives  104 us (34%)
  waiting for transfers between devices  100 us (33%)
  Pallas kernels  59.9 us (20%)
  local copies, waits for them, and re-layouts  13.8 us (5%)
  between operations  13.5 us (4%)
  starting transfers between devices  10.7 us (4%)
    all_to_all x1, blocking collectives, on_device_chunks(): lax.all_to_all(spectra, ('chan', 'tm'), split_axis=0, concat_axis=0, tile...  53.9 us
    all_to_all x1, blocking collectives, on_device_chunks(): lax.all_to_all(sending, 'tm', split_axis=0, concat_axis=0, tiled=True)  50.2 us
    all_to_all x1, waiting for transfers between devices, on_device_chunks(): lax.all_to_all(spectra, ('chan', 'tm'), split_axis=0, concat_axis=0, tile...  42.6 us
    all_to_all x1, waiting for transfers between devices, on_device_chunks(): lax.all_to_all(sending, 'tm', split_axis=0, concat_axis=0, tiled=True)  42.1 us
    pallas_call x2, Pallas kernels, channelise(): pl.pallas_call(lambda *refs: channelise_kernel(frames, *refs), out_shape=...  31.1 us
    pallas_call x1, Pallas kernels, correlate_tiles(): pl.pallas_call(lambda *refs: correlate_kernel(len(chunks), width, *refs),...  28.8 us
    all_gather x2, waiting for transfers between devices, on_device_chunks(): received.append(lax.all_gather(moved, 'pol', axis=0, tiled=False))  14.5 us
    unnamed x22, local copies, waits for them, and re-layouts  9.65 us
  transfers between devices with their start and end apart: 4, of which 3 were waited for; matrix products, arithmetic and copies ran while one was open for 1% of the time, Pallas kernels for 5%

commit v1 on v0

--- a/solution.py
+++ b/solution.py
@@ -178,10 +178,24 @@
     return first + second
 
 
-def channelise_kernel(
-    frames, x_ref, taps_ref, twiddle_ref, matrix_ref, out_ref, fil_ref, zr_ref, zi_ref, w_ref
-):
-    sources = x_ref.shape[0]
+def channelise_kernel(frames, chunk, place_ref, own_ref, *refs):
+    sources = refs[-6].shape[0]
+    come_refs = refs[: sources - 1]
+    taps_ref, twiddle_ref, matrix_ref = refs[sources - 1 : sources + 2]
+    out_refs = refs[sources + 2 : -6]
+    x_ref, fil_ref, zr_ref, zi_ref, w_ref, sems = refs[-6:]
+    chan, tm = place_ref[0], place_ref[1]
+    columns = len(out_refs) // sources
+    own_rows = pl.multiple_of((tm * (own_ref.shape[1] // (sources * ROWS)) + chunk) * ROWS, ROWS)
+    copies = []
+    for behind in range(sources):
+        block = come_refs[behind - 1] if behind else own_ref.at[:, pl.ds(own_rows, ROWS), :]
+        slot = lax.rem(tm - behind + sources, sources)
+        copies.append(pltpu.make_async_copy(block, x_ref.at[slot], sems.at[behind]))
+    for copy in copies:
+        copy.start()
+    for copy in copies:
+        copy.wait()
     spectra = sources * frames
     length = taps_ref.shape[1]
     taps = taps_ref.shape[0]
@@ -240,38 +254,45 @@
                 ]
 
     piece = 256
-
-    @pl.loop(0, out_ref.shape[0] // piece)
-    def _(index):
-        rows = pl.ds(pl.multiple_of(index * piece, piece), piece)
-        out_ref[rows, :] = w_ref[rows, :].astype(jnp.bfloat16)
-
-
-def channelise(blocks, taps_filter, tables, frames):
-    sources = blocks.shape[0]
+    share = out_refs[0].shape[0]
+    for number, out_ref in enumerate(out_refs):
+        column = lax.rem(chan + number // sources, columns)
+        owner = column * sources + lax.rem(tm + number % sources, sources)
+        for step in range(share // piece):
+            rows = pl.ds(pl.multiple_of(owner * share + step * piece, piece), piece)
+            out_ref[step * piece : (step + 1) * piece, :] = w_ref[rows, :].astype(jnp.bfloat16)
+
+
+def channelise(place, chunk, voltages, come, taps_filter, tables, frames, owners):
+    sources = 1 + len(come)
     length = taps_filter.shape[1]
     spectra = sources * frames
     twiddle, matrix = tables
     out_rows = length // AVG * 2 * ROWS
     whole = pl.BlockSpec(memory_space=pltpu.VMEM)
+    share = out_rows // owners
     flat = pl.pallas_call(
-        lambda *refs: channelise_kernel(frames, *refs),
-        out_shape=jax.ShapeDtypeStruct((out_rows, LANES), jnp.bfloat16),
-        in_specs=[whole] * 4,
-        out_specs=whole,
+        lambda *refs: channelise_kernel(frames, chunk, *refs),
+        out_shape=[jax.ShapeDtypeStruct((share, LANES), jnp.bfloat16)] * owners,
+        in_specs=[pl.BlockSpec(memory_space=pltpu.SMEM)]
+        + [pl.BlockSpec(memory_space=pl.ANY)] * sources
+        + [whole] * 3,
+        out_specs=[whole] * owners,
         scratch_shapes=[
+            pltpu.VMEM((sources, 2, ROWS, frames * length), jnp.bfloat16),
             pltpu.VMEM((RADIX, spectra, 2, ROWS, LANES), jnp.float32),
             pltpu.VMEM((ROWS * RADIX * spectra, LANES), jnp.float32),
             pltpu.VMEM((ROWS * RADIX * spectra, LANES), jnp.float32),
             pltpu.VMEM((out_rows, LANES), jnp.float32),
+            pltpu.SemaphoreType.DMA((sources,)),
         ],
         compiler_params=pltpu.CompilerParams(vmem_limit_bytes=40 * 2**20),
         cost_estimate=pl.CostEstimate(
             flops=9 * 10**9, bytes_accessed=4 * 2**20, transcendentals=0
         ),
         name="channelise",
-    )(blocks, taps_filter, jnp.asarray(twiddle), jnp.asarray(matrix))
-    return flat.reshape(length // AVG, 2, ROWS, LANES)
+    )(place, voltages, *come, taps_filter, jnp.asarray(twiddle), jnp.asarray(matrix))
+    return [piece.reshape(length // AVG // owners, 2, ROWS, LANES) for piece in flat]
 
 
 def correlate_kernel(chunks, width, *refs):
@@ -371,12 +392,16 @@
     bands = length // AVG // owners
     tables = fourier_tables(length)
 
+    chan, tm = lax.axis_index("chan"), lax.axis_index("tm")
+    place = jnp.stack([chan, tm]).astype(jnp.int32)
+
     def row_of(station):
-        column = station // stations
-        rest = station % stations
+        column, rest = station // stations, station % stations
         block, inside = rest // (chunk_count * ROWS), rest % (chunk_count * ROWS)
-        source = column * time_count + block
-        return (inside // ROWS) * (owners * ROWS) + source * ROWS + inside % ROWS
+        across = (chan - column) % chan_count
+        behind = (tm - block) % time_count
+        piece = across * time_count + behind
+        return ((inside // ROWS) * owners + piece) * ROWS + inside % ROWS
 
     rows, flags = tile_tables(tile_a, tile_b, tile_owner, tile_flags, row_of)
     total_rows = chunk_count * owners * ROWS
@@ -385,14 +410,36 @@
     depth = AVG * time_count * frames
     weight = jnp.tile(flags * (1.0 / depth), (1, 4 * AVG))
 
-    pieces = voltages.reshape(2, time_count, chunk_count, ROWS, frames * length)
+    samples = voltages.reshape(2, stations, frames * length)
+
+    def ahead(value, across, along):
+        pairs = [
+            (x * time_count + z, (x + across) % chan_count * time_count + (z + along) % time_count)
+            for x in range(chan_count)
+            for z in range(time_count)
+        ]
+        return lax.ppermute(value, ("chan", "tm"), pairs)
+
+    def block_for(chunk, along):
+        first = ((tm + along) % time_count * chunk_count + chunk) * ROWS
+        return lax.dynamic_slice(samples, (0, first, 0), (2, ROWS, frames * length))
+
+    come = [
+        [ahead(block_for(chunk, along), 0, along) for along in range(1, time_count)]
+        for chunk in range(chunk_count)
+    ]
     received = []
     for chunk in range(chunk_count):
-        sending = pieces[:, :, chunk].transpose(1, 0, 2, 3)
-        blocks = lax.all_to_all(sending, "tm", split_axis=0, concat_axis=0, tiled=True)
-        spectra = channelise(blocks, taps_filter, tables, frames)
-        spectra = spectra.reshape(owners, bands, 2, ROWS, LANES)
-        moved = lax.all_to_all(spectra, ("chan", "tm"), split_axis=0, concat_axis=0, tiled=True)
+        spectra = channelise(
+            place, chunk, samples, come[chunk], taps_filter, tables, frames, owners
+        )
+        moved = jnp.stack(
+            spectra[:1]
+            + [
+                ahead(spectra[owner], owner // time_count, owner % time_count)
+                for owner in range(1, owners)
+            ]
+        )
         received.append(lax.all_gather(moved, "pol", axis=0, tiled=False))
     return correlate_tiles(received, select, weight, width)
 

time: 304 us -> 293 us (0.964)
  blocking collectives: 104 us -> 0 us
  waiting for transfers between devices: 100 us -> 171 us
  starting transfers between devices: 10.7 us -> 26.6 us
  local copies, waits for them, and re-layouts: 13.8 us -> 19.7 us
    ppermute x0 -> x20, waiting for transfers between devices: none -> 157 us  [ahead(): return lax.ppermute(value, ('chan', 'tm'), pairs)]
    all_to_all x2 -> x0, blocking collectives: 104 us -> none  [the longest x1 53.9 us: on_device_chunks(): lax.all_to_all(spectra, ('chan', 'tm'), split_axis=0, concat_axis=0, tile...]
    all_to_all x2 -> x0, waiting for transfers between devices: 84.8 us -> none  [the longest x1 42.6 us: on_device_chunks(): lax.all_to_all(spectra, ('chan', 'tm'), split_axis=0, concat_axis=0, tile...]
    ppermute x0 -> x20, starting transfers between devices: none -> 26.6 us  [ahead(): return lax.ppermute(value, ('chan', 'tm'), pairs)]
    all_to_all x2 -> x0, starting transfers between devices: 10.6 us -> none  [the longest x1 6.02 us: on_device_chunks(): lax.all_to_all(spectra, ('chan', 'tm'), split_axis=0, concat_axis=0, tile...]
    unnamed x22 -> x40, local copies, waits for them, and re-layouts: 9.65 us -> 15.4 us
    slice x1 -> x0, local copies, waits for them, and re-layouts: 3.98 us -> none  [on_device_chunks(): sending = pieces[:, :, chunk].transpose(1, 0, 2, 3)]
    dynamic_slice x0 -> x1, local copies, waits for them, and re-layouts: none -> 3.31 us  [block_for(): return lax.dynamic_slice(samples, (0, first, 0), (2, ROWS, frames * length))]
  transfers between devices with their start and end apart: 4 -> 22, of which waited for: 3 -> 18; matrix products, arithmetic and copies ran while one was open for 1% -> 2% of each run, Pallas kernels for 5% -> 5%
where the time goes in v1:
time: 293 us; the launch traced here: 292 us
  waiting for transfers between devices  171 us (58%)
  Pallas kernels  59.9 us (20%)
  starting transfers between devices  26.6 us (9%)
  local copies, waits for them, and re-layouts  19.7 us (7%)
  between operations  13.7 us (5%)
    ppermute x20, waiting for transfers between devices, ahead(): return lax.ppermute(value, ('chan', 'tm'), pairs)  157 us
    pallas_call x2, Pallas kernels, channelise(): pl.pallas_call(lambda *refs: channelise_kernel(frames, chunk, *refs), out...  31.1 us
    pallas_call x1, Pallas kernels, correlate_tiles(): pl.pallas_call(lambda *refs: correlate_kernel(len(chunks), width, *refs),...  28.8 us
    ppermute x20, starting transfers between devices, ahead(): return lax.ppermute(value, ('chan', 'tm'), pairs)  26.6 us
    unnamed x40, local copies, waits for them, and re-layouts  15.4 us
    all_gather x2, waiting for transfers between devices, on_device_chunks(): received.append(lax.all_gather(moved, 'pol', axis=0, tiled=False))  14.3 us
  transfers between devices with their start and end apart: 22, of which 18 were waited for; matrix products, arithmetic and copies ran while one was open for 2% of the time, Pallas kernels for 5%

profile of v1, /device:TPU:11, one launch (start us, length us, event | category | flops | bytes accessed | tf_op | source)
XLA Modules:
  0.0 291.7 jit_solution(11621090568394136519)
XLA Ops:
  6.5 3.3 %dynamic-slice_bitcast_fusion = (bf16[2,16,8192]{2,1,0:T(8,128)(2,1)}, bf16[2,16,8192]{2,1,0:T(8,128)(2,1)}, bf16[2,16,8192]{2,1,0:T(8,128)(2,1)}, bf16[2,16,819...) fusion(bf16[2,1,128,8192]{3,2,1,0:T(8,128)(2,1)} %param.8, s32[]{:T(128)S(6)} %select_n.125, ...), kind=kLoop, calls=%fused_computation.2 | loop fusion | bytes 6291480 | tf_op jit(solution)/shard_map/dynamic_slice | solution.py:425
  11.3 4.1 %collective-permute-start.11 = (bf16[2,16,8192]{2,1,0:T(8,128)(2,1)}, bf16[2,16,8192]{2,1,0:T(8,128)(2,1)S(1)}, u32[]{:S(2)}, u32[]{:S(2)}) collective-permute-start(bf16[2,16,8192]{2,1,0:T(8,128)(2,1)} %get-tuple-element.42), channel_id=1, source_target_pairs={{0,4},{2,6},{4,0},{6,2},{8,12},{10,14},{12,8},{14,10},{1,5},{3,7},... | collective-permute-start | bytes 1572872 | tf_op jit(solution)/shard_map/ppermute | solution.py:421
  15.5 7.4 %collective-permute-done.12.refs_4_ = bf16[2,16,8192]{2,1,0:T(8,128)(2,1)S(1)} collective-permute-done((bf16[2,16,8192]{2,1,0:T(8,128)(2,1)}, bf16[2,16,8192]{2,1,0:T(8,128)(2,1)S(1)}, u32[]{:S(2)}, u32[]{:S(2)}) %collective-permute-start.12) | collective-permute-done | bytes 524320 | tf_op jit(solution)/shard_map/ppermute | solution.py:421
  22.9 13.3 %collective-permute-done.10.refs_2_ = bf16[2,16,8192]{2,1,0:T(8,128)(2,1)S(1)} collective-permute-done((bf16[2,16,8192]{2,1,0:T(8,128)(2,1)}, bf16[2,16,8192]{2,1,0:T(8,128)(2,1)S(1)}, u32[]{:S(2)}, u32[]{:S(2)}) %collective-permute-start.10) | collective-permute-done | bytes 524320 | tf_op jit(solution)/shard_map/ppermute | solution.py:421
  36.2 19.4 %collective-permute-done.11.refs_3_ = bf16[2,16,8192]{2,1,0:T(8,128)(2,1)S(1)} collective-permute-done((bf16[2,16,8192]{2,1,0:T(8,128)(2,1)}, bf16[2,16,8192]{2,1,0:T(8,128)(2,1)S(1)}, u32[]{:S(2)}, u32[]{:S(2)}) %collective-permute-start.11) | collective-permute-done | bytes 524320 | tf_op jit(solution)/shard_map/ppermute | solution.py:421
  57.8 15.5 %channelise.3 = (bf16[1024,128]{1,0:T(8,128)(2,1)S(1)}, bf16[1024,128]{1,0:T(8,128)(2,1)S(1)}, bf16[1024,128]{1,0:T(8,128)(2,1)S(1)}, bf16[1024,128]{1,0:T(8,128...) custom-call(s32[2]{0:T(128)S(1)} %pad_add_fusion.refs_0_, ...), custom_call_target="tpu_custom_call" | custom-call | flops 8999999488 | bytes 4194304 | tf_op jit(solution)/shard_map/channelise/pallas_call | solution.py:274
  73.7 3.9 %collective-permute-start.14 = (bf16[32,2,16,128]{3,2,1,0:T(8,128)(2,1)S(1)}, bf16[32,2,16,128]{3,2,1,0:T(8,128)(2,1)S(1)}, u32[]{:S(2)}, u32[]{:S(2)}) collective-permute-start(bf16[32,2,16,128]{3,2,1,0:T(8,128)(2,1)S(1)} %bitcast.82), channel_id=1, source_target_pairs={{0,4},{2,6},{4,0},{6,2},{8,12},{10,14},{12,8},{14,10},{1,5},{3,7},... | collective-permute-start | bytes 786440 | tf_op jit(solution)/shard_map/ppermute | solution.py:421
  81.0 2.2 collective-permute-start.18
  84.0 11.0 %collective-permute-done.14 = bf16[32,2,16,128]{3,2,1,0:T(8,128)(2,1)S(1)} collective-permute-done((bf16[32,2,16,128]{3,2,1,0:T(8,128)(2,1)S(1)}, bf16[32,2,16,128]{3,2,1,0:T(8,128)(2,1)S(1)}, u32[]{:S(2)}, u32[]{:S(2)}) %collective-permute-start.14) | collective-permute-done | bytes 262176 | tf_op jit(solution)/shard_map/ppermute | solution.py:421
  96.0 14.8 %collective-permute-done.15 = bf16[32,2,16,128]{3,2,1,0:T(8,128)(2,1)S(1)} collective-permute-done((bf16[32,2,16,128]{3,2,1,0:T(8,128)(2,1)S(1)}, bf16[32,2,16,128]{3,2,1,0:T(8,128)(2,1)S(1)}, u32[]{:S(2)}, u32[]{:S(2)}) %collective-permute-start.15) | collective-permute-done | bytes 262176 | tf_op jit(solution)/shard_map/ppermute | solution.py:421
  113.6 4.8 %collective-permute-done.18 = bf16[32,2,16,128]{3,2,1,0:T(8,128)(2,1)S(1)} collective-permute-done((bf16[32,2,16,128]{3,2,1,0:T(8,128)(2,1)S(1)}, bf16[32,2,16,128]{3,2,1,0:T(8,128)(2,1)S(1)}, u32[]{:S(2)}, u32[]{:S(2)}) %collective-permute-start.18) | collective-permute-done | bytes 262176 | tf_op jit(solution)/shard_map/ppermute | solution.py:421
  119.2 2.9 collective-permute-done.19
  125.5 10.7 %collective-permute-done.2.refs_4_ = bf16[2,16,8192]{2,1,0:T(8,128)(2,1)S(1)} collective-permute-done((bf16[2,16,8192]{2,1,0:T(8,128)(2,1)S(1)}, bf16[2,16,8192]{2,1,0:T(8,128)(2,1)S(1)}, u32[]{:S(2)}, u32[]{:S(2)}) %collective-permute-start.2) | collective-permute-done | bytes 524320 | tf_op jit(solution)/shard_map/ppermute | solution.py:421
  136.2 20.6 %collective-permute-done.1.refs_3_ = bf16[2,16,8192]{2,1,0:T(8,128)(2,1)S(1)} collective-permute-done((bf16[2,16,8192]{2,1,0:T(8,128)(2,1)S(1)}, bf16[2,16,8192]{2,1,0:T(8,128)(2,1)S(1)}, u32[]{:S(2)}, u32[]{:S(2)}) %collective-permute-start.1) | collective-permute-done | bytes 524320 | tf_op jit(solution)/shard_map/ppermute | solution.py:421
  156.8 11.2 %collective-permute-done.refs_2_ = bf16[2,16,8192]{2,1,0:T(8,128)(2,1)S(1)} collective-permute-done((bf16[2,16,8192]{2,1,0:T(8,128)(2,1)S(1)}, bf16[2,16,8192]{2,1,0:T(8,128)(2,1)S(1)}, u32[]{:S(2)}, u32[]{:S(2)}) %collective-permute-start) | collective-permute-done | bytes 524320 | tf_op jit(solution)/shard_map/ppermute | solution.py:421
  170.2 15.5 %channelise.2 = (bf16[1024,128]{1,0:T(8,128)(2,1)S(1)}, bf16[1024,128]{1,0:T(8,128)(2,1)S(1)}, bf16[1024,128]{1,0:T(8,128)(2,1)S(1)}, bf16[1024,128]{1,0:T(8,128...) custom-call(s32[2]{0:T(128)S(1)} %pad_add_fusion.refs_0_, ...), custom_call_target="tpu_custom_call" | custom-call | flops 8999999488 | bytes 4194304 | tf_op jit(solution)/shard_map/channelise/pallas_call | solution.py:274
  185.7 2.3 collective-permute-start.3
  193.2 2.3 collective-permute-start.8
  195.6 14.5 %collective-permute-done.4 = bf16[32,2,16,128]{3,2,1,0:T(8,128)(2,1)S(1)} collective-permute-done((bf16[32,2,16,128]{3,2,1,0:T(8,128)(2,1)S(1)}, bf16[32,2,16,128]{3,2,1,0:T(8,128)(2,1)S(1)}, u32[]{:S(2)}, u32[]{:S(2)}) %collective-permute-start.4) | collective-permute-done | bytes 262176 | tf_op jit(solution)/shard_map/ppermute | solution.py:421
  210.1 12.8 %collective-permute-done.5 = bf16[32,2,16,128]{3,2,1,0:T(8,128)(2,1)S(1)} collective-permute-done((bf16[32,2,16,128]{3,2,1,0:T(8,128)(2,1)S(1)}, bf16[32,2,16,128]{3,2,1,0:T(8,128)(2,1)S(1)}, u32[]{:S(2)}, u32[]{:S(2)}) %collective-permute-start.5) | collective-permute-done | bytes 262176 | tf_op jit(solution)/shard_map/ppermute | solution.py:421
  223.3 8.4 %collective-permute-done.8 = bf16[32,2,16,128]{3,2,1,0:T(8,128)(2,1)S(1)} collective-permute-done((bf16[32,2,16,128]{3,2,1,0:T(8,128)(2,1)S(1)}, bf16[32,2,16,128]{3,2,1,0:T(8,128)(2,1)S(1)}, u32[]{:S(2)}, u32[]{:S(2)}) %collective-permute-start.8) | collective-permute-done | bytes 262176 | tf_op jit(solution)/shard_map/ppermute | solution.py:421
  231.7 3.4 %collective-permute-done.9 = bf16[32,2,16,128]{3,2,1,0:T(8,128)(2,1)S(1)} collective-permute-done((bf16[32,2,16,128]{3,2,1,0:T(8,128)(2,1)S(1)}, bf16[32,2,16,128]{3,2,1,0:T(8,128)(2,1)S(1)}, u32[]{:S(2)}, u32[]{:S(2)}) %collective-permute-start.9) | collective-permute-done | bytes 262176 | tf_op jit(solution)/shard_map/ppermute | solution.py:421
  237.5 14.3 %all-gather.5.cloned.1.call-done = bf16[16,32,2,16,128]{4,3,2,1,0:T(8,128)(2,1)} async-done(((bf16[8,32,2,16,128]{4,3,2,1,0:T(8,128)(2,1)}), bf16[16,32,2,16,128]{4,3,2,1,0:T(8,128)(2,1)}) %all-gather.5.cloned.1.call-update) | async-done | bytes 4194320 | tf_op jit(solution)/shard_map/all_gather | solution.py:443
  256.1 28.8 %correlate.1 = f32[8,32,2,2,64,128]{5,4,3,2,1,0:T(8,128)} custom-call(bf16[1024,256]{1,0:T(8,128)(2,1)S(1)} %fusion.refs_0_, f32[8,512]{1,0:T(8,128)S(1)} %tile.10.refs_1_, bf16[2,8,32,2,16,128]{5,4,3,2,1,0:T(8,128)(2,1)S(1)} %bitcast.70, bf16[2,8,32,2,16,128]{5,4,3,2,1,0:T(8,128)(2,1)S(1)} %bitcast.69), custom_call_target="tpu_custom_call" | custom-call | flops 12999999488 | bytes 44040192 | tf_op jit(solution)/shard_map/correlate/pallas_call | solution.py:347
  (84 shorter events, 30.7 us)
Async XLA Ops:
  6.5 230.9 %all-gather.7.cloned.1.call-start = ((), (), s32[]{:S(2)}) async-start(), calls=%async_computation.1 | async-start | bytes 6291456 | tf_op jit(solution)/shard_map/all_gather | solution.py:443
  6.5 49.1 %copy-start.5 = (bf16[2,256,256]{2,1,0:T(8,128)(2,1)S(1)}, bf16[2,256,256]{2,1,0:T(8,128)(2,1)}, u32[]{:S(2)}) copy-start(bf16[2,256,256]{2,1,0:T(8,128)(2,1)} %constant.191.clone.refs_7_) | copy-start | bytes 786436
  6.5 49.1 %copy-start.6 = (f32[2,16,128]{2,1,0:T(8,128)S(1)}, f32[2,16,128]{2,1,0:T(8,128)}, u32[]{:S(2)}) copy-start(f32[2,16,128]{2,1,0:T(8,128)} %constant.190.clone.refs_6_) | copy-start | bytes 49156
  9.9 13.0 %collective-permute-start.12 = (bf16[2,16,8192]{2,1,0:T(8,128)(2,1)}, bf16[2,16,8192]{2,1,0:T(8,128)(2,1)S(1)}, u32[]{:S(2)}, u32[]{:S(2)}) collective-permute-start(bf16[2,16,8192]{2,1,0:T(8,128)(2,1)} %get-tuple-element.37), channel_id=1, source_target_pairs={{0,6},{2,0},{4,2},{6,4},{8,14},{10,8},{12,10},{14,12},{1,7},{3,1},... | collective-permute-start | bytes 1572872 | tf_op jit(solution)/shard_map/ppermute | solution.py:421
  10.0 26.2 %collective-permute-start.10 = (bf16[2,16,8192]{2,1,0:T(8,128)(2,1)}, bf16[2,16,8192]{2,1,0:T(8,128)(2,1)S(1)}, u32[]{:S(2)}, u32[]{:S(2)}) collective-permute-start(bf16[2,16,8192]{2,1,0:T(8,128)(2,1)} %get-tuple-element.38), channel_id=1, source_target_pairs={{0,2},{2,4},{4,6},{6,0},{8,10},{10,12},{12,14},{14,8},{1,3},{3,5},... | collective-permute-start | bytes 1572872 | tf_op jit(solution)/shard_map/ppermute | solution.py:421
  11.3 44.3 %collective-permute-start.11 = (bf16[2,16,8192]{2,1,0:T(8,128)(2,1)}, bf16[2,16,8192]{2,1,0:T(8,128)(2,1)S(1)}, u32[]{:S(2)}, u32[]{:S(2)}) collective-permute-start(bf16[2,16,8192]{2,1,0:T(8,128)(2,1)} %get-tuple-element.42), channel_id=1, source_target_pairs={{0,4},{2,6},{4,0},{6,2},{8,12},{10,14},{12,8},{14,10},{1,5},{3,7},... | collective-permute-start | bytes 1572872 | tf_op jit(solution)/shard_map/ppermute | solution.py:421
  73.4 7.7 %collective-permute-start.13 = (bf16[32,2,16,128]{3,2,1,0:T(8,128)(2,1)S(1)}, bf16[32,2,16,128]{3,2,1,0:T(8,128)(2,1)S(1)}, u32[]{:S(2)}, u32[]{:S(2)}) collective-permute-start(bf16[32,2,16,128]{3,2,1,0:T(8,128)(2,1)S(1)} %bitcast.84), channel_id=1, source_target_pairs={{0,2},{2,4},{4,6},{6,0},{8,10},{10,12},{12,14},{14,8},{1,3},{3,5},... | collective-permute-start | bytes 786440 | tf_op jit(solution)/shard_map/ppermute | solution.py:421
  73.7 21.2 %collective-permute-start.14 = (bf16[32,2,16,128]{3,2,1,0:T(8,128)(2,1)S(1)}, bf16[32,2,16,128]{3,2,1,0:T(8,128)(2,1)S(1)}, u32[]{:S(2)}, u32[]{:S(2)}) collective-permute-start(bf16[32,2,16,128]{3,2,1,0:T(8,128)(2,1)S(1)} %bitcast.82), channel_id=1, source_target_pairs={{0,4},{2,6},{4,0},{6,2},{8,12},{10,14},{12,8},{14,10},{1,5},{3,7},... | collective-permute-start | bytes 786440 | tf_op jit(solution)/shard_map/ppermute | solution.py:421
  77.6 33.2 %collective-permute-start.15 = (bf16[32,2,16,128]{3,2,1,0:T(8,128)(2,1)S(1)}, bf16[32,2,16,128]{3,2,1,0:T(8,128)(2,1)S(1)}, u32[]{:S(2)}, u32[]{:S(2)}) collective-permute-start(bf16[32,2,16,128]{3,2,1,0:T(8,128)(2,1)S(1)} %bitcast.80), channel_id=1, source_target_pairs={{0,6},{2,0},{4,2},{6,4},{8,14},{10,8},{12,10},{14,12},{1,7},{3,1},... | collective-permute-start | bytes 786440 | tf_op jit(solution)/shard_map/ppermute | solution.py:421
  77.9 33.7 %collective-permute-start.16 = (bf16[32,2,16,128]{3,2,1,0:T(8,128)(2,1)S(1)}, bf16[32,2,16,128]{3,2,1,0:T(8,128)(2,1)S(1)}, u32[]{:S(2)}, u32[]{:S(2)}) collective-permute-start(bf16[32,2,16,128]{3,2,1,0:T(8,128)(2,1)S(1)} %bitcast.78), channel_id=1, source_target_pairs={{0,8},{2,10},{4,12},{6,14},{8,0},{10,2},{12,4},{14,6},{1,9},{3,11}... | collective-permute-start | bytes 786440 | tf_op jit(solution)/shard_map/ppermute | solution.py:421
  78.1 34.8 %collective-permute-start.17 = (bf16[32,2,16,128]{3,2,1,0:T(8,128)(2,1)S(1)}, bf16[32,2,16,128]{3,2,1,0:T(8,128)(2,1)S(1)}, u32[]{:S(2)}, u32[]{:S(2)}) collective-permute-start(bf16[32,2,16,128]{3,2,1,0:T(8,128)(2,1)S(1)} %bitcast.76), channel_id=1, source_target_pairs={{0,10},{2,12},{4,14},{6,8},{8,2},{10,4},{12,6},{14,0},{1,11},{3,13... | collective-permute-start | bytes 786440 | tf_op jit(solution)/shard_map/ppermute | solution.py:421
  81.0 37.4 %collective-permute-start.18 = (bf16[32,2,16,128]{3,2,1,0:T(8,128)(2,1)S(1)}, bf16[32,2,16,128]{3,2,1,0:T(8,128)(2,1)S(1)}, u32[]{:S(2)}, u32[]{:S(2)}) collective-permute-start(bf16[32,2,16,128]{3,2,1,0:T(8,128)(2,1)S(1)} %bitcast.74), channel_id=1, source_target_pairs={{0,12},{2,14},{4,8},{6,10},{8,4},{10,6},{12,0},{14,2},{1,13},{3,15... | collective-permute-start | bytes 786440 | tf_op jit(solution)/shard_map/ppermute | solution.py:421
  95.0 27.1 %collective-permute-start.19 = (bf16[32,2,16,128]{3,2,1,0:T(8,128)(2,1)S(1)}, bf16[32,2,16,128]{3,2,1,0:T(8,128)(2,1)S(1)}, u32[]{:S(2)}, u32[]{:S(2)}) collective-permute-start(bf16[32,2,16,128]{3,2,1,0:T(8,128)(2,1)S(1)} %bitcast.72), channel_id=1, source_target_pairs={{0,14},{2,8},{4,10},{6,12},{8,6},{10,0},{12,2},{14,4},{1,15},{3,9}... | collective-permute-start | bytes 786440 | tf_op jit(solution)/shard_map/ppermute | solution.py:421
  122.8 128.9 %all-gather.5.cloned.1.call-start = ((), (), s32[]{:S(2)}) async-start(), calls=%async_computation | async-start | bytes 6291456 | tf_op jit(solution)/shard_map/all_gather | solution.py:443
  122.9 13.3 %collective-permute-start.2 = (bf16[2,16,8192]{2,1,0:T(8,128)(2,1)S(1)}, bf16[2,16,8192]{2,1,0:T(8,128)(2,1)S(1)}, u32[]{:S(2)}, u32[]{:S(2)}) collective-permute-start(bf16[2,16,8192]{2,1,0:T(8,128)(2,1)S(1)} %copy-done.8), channel_id=1, source_target_pairs={{0,6},{2,0},{4,2},{6,4},{8,14},{10,8},{12,10},{14,12},{1,7},{3,1},... | collective-permute-start | bytes 1572872 | tf_op jit(solution)/shard_map/ppermute | solution.py:421
  122.9 33.8 %collective-permute-start.1 = (bf16[2,16,8192]{2,1,0:T(8,128)(2,1)S(1)}, bf16[2,16,8192]{2,1,0:T(8,128)(2,1)S(1)}, u32[]{:S(2)}, u32[]{:S(2)}) collective-permute-start(bf16[2,16,8192]{2,1,0:T(8,128)(2,1)S(1)} %get-tuple-element.40), channel_id=1, source_target_pairs={{0,4},{2,6},{4,0},{6,2},{8,12},{10,14},{12,8},{14,10},{1,5},{3,7},... | collective-permute-start | bytes 1572872 | tf_op jit(solution)/shard_map/ppermute | solution.py:421
  123.4 44.6 %collective-permute-start = (bf16[2,16,8192]{2,1,0:T(8,128)(2,1)S(1)}, bf16[2,16,8192]{2,1,0:T(8,128)(2,1)S(1)}, u32[]{:S(2)}, u32[]{:S(2)}) collective-permute-start(bf16[2,16,8192]{2,1,0:T(8,128)(2,1)S(1)} %get-tuple-element.41), channel_id=1, source_target_pairs={{0,2},{2,4},{4,6},{6,0},{8,10},{10,12},{12,14},{14,8},{1,3},{3,5},... | collective-permute-start | bytes 1572872 | tf_op jit(solution)/shard_map/ppermute | solution.py:421
  185.7 7.5 %collective-permute-start.3 = (bf16[32,2,16,128]{3,2,1,0:T(8,128)(2,1)S(1)}, bf16[32,2,16,128]{3,2,1,0:T(8,128)(2,1)S(1)}, u32[]{:S(2)}, u32[]{:S(2)}) collective-permute-start(bf16[32,2,16,128]{3,2,1,0:T(8,128)(2,1)S(1)} %bitcast.83), channel_id=1, source_target_pairs={{0,2},{2,4},{4,6},{6,0},{8,10},{10,12},{12,14},{14,8},{1,3},{3,5},... | collective-permute-start | bytes 786440 | tf_op jit(solution)/shard_map/ppermute | solution.py:421
  188.0 22.1 %collective-permute-start.4 = (bf16[32,2,16,128]{3,2,1,0:T(8,128)(2,1)S(1)}, bf16[32,2,16,128]{3,2,1,0:T(8,128)(2,1)S(1)}, u32[]{:S(2)}, u32[]{:S(2)}) collective-permute-start(bf16[32,2,16,128]{3,2,1,0:T(8,128)(2,1)S(1)} %bitcast.81), channel_id=1, source_target_pairs={{0,4},{2,6},{4,0},{6,2},{8,12},{10,14},{12,8},{14,10},{1,5},{3,7},... | collective-permute-start | bytes 786440 | tf_op jit(solution)/shard_map/ppermute | solution.py:421
  189.7 33.2 %collective-permute-start.5 = (bf16[32,2,16,128]{3,2,1,0:T(8,128)(2,1)S(1)}, bf16[32,2,16,128]{3,2,1,0:T(8,128)(2,1)S(1)}, u32[]{:S(2)}, u32[]{:S(2)}) collective-permute-start(bf16[32,2,16,128]{3,2,1,0:T(8,128)(2,1)S(1)} %bitcast.79), channel_id=1, source_target_pairs={{0,6},{2,0},{4,2},{6,4},{8,14},{10,8},{12,10},{14,12},{1,7},{3,1},... | collective-permute-start | bytes 786440 | tf_op jit(solution)/shard_map/ppermute | solution.py:421
  189.7 33.3 %collective-permute-start.6 = (bf16[32,2,16,128]{3,2,1,0:T(8,128)(2,1)S(1)}, bf16[32,2,16,128]{3,2,1,0:T(8,128)(2,1)S(1)}, u32[]{:S(2)}, u32[]{:S(2)}) collective-permute-start(bf16[32,2,16,128]{3,2,1,0:T(8,128)(2,1)S(1)} %bitcast.77), channel_id=1, source_target_pairs={{0,8},{2,10},{4,12},{6,14},{8,0},{10,2},{12,4},{14,6},{1,9},{3,11}... | collective-permute-start | bytes 786440 | tf_op jit(solution)/shard_map/ppermute | solution.py:421
  190.9 32.3 %collective-permute-start.7 = (bf16[32,2,16,128]{3,2,1,0:T(8,128)(2,1)S(1)}, bf16[32,2,16,128]{3,2,1,0:T(8,128)(2,1)S(1)}, u32[]{:S(2)}, u32[]{:S(2)}) collective-permute-start(bf16[32,2,16,128]{3,2,1,0:T(8,128)(2,1)S(1)} %bitcast.75), channel_id=1, source_target_pairs={{0,10},{2,12},{4,14},{6,8},{8,2},{10,4},{12,6},{14,0},{1,11},{3,13... | collective-permute-start | bytes 786440 | tf_op jit(solution)/shard_map/ppermute | solution.py:421
  193.2 38.4 %collective-permute-start.8 = (bf16[32,2,16,128]{3,2,1,0:T(8,128)(2,1)S(1)}, bf16[32,2,16,128]{3,2,1,0:T(8,128)(2,1)S(1)}, u32[]{:S(2)}, u32[]{:S(2)}) collective-permute-start(bf16[32,2,16,128]{3,2,1,0:T(8,128)(2,1)S(1)} %bitcast.73), channel_id=1, source_target_pairs={{0,12},{2,14},{4,8},{6,10},{8,4},{10,6},{12,0},{14,2},{1,13},{3,15... | collective-permute-start | bytes 786440 | tf_op jit(solution)/shard_map/ppermute | solution.py:421
  210.1 25.0 %collective-permute-start.9 = (bf16[32,2,16,128]{3,2,1,0:T(8,128)(2,1)S(1)}, bf16[32,2,16,128]{3,2,1,0:T(8,128)(2,1)S(1)}, u32[]{:S(2)}, u32[]{:S(2)}) collective-permute-start(bf16[32,2,16,128]{3,2,1,0:T(8,128)(2,1)S(1)} %bitcast.71), channel_id=1, source_target_pairs={{0,14},{2,8},{4,10},{6,12},{8,6},{10,0},{12,2},{14,4},{1,15},{3,9}... | collective-permute-start | bytes 786440 | tf_op jit(solution)/shard_map/ppermute | solution.py:421
  (11 other events, 125.1 us)
Sparse Core Ops, SparseCore 0:
  122.9 14.8 all-gather.6
  236.6 15.1 all-gather.4
